TPU v7x, 32 devices: a whole 2x2x4 slice. The times are simulated.
32 devices in a mesh: grp: 4 (over y, x), tp: 8 (over z, core).
Axes of the slice: x: 2, y: 2, z: 4, core: 2. Of those that a mesh axis runs over, the one named last changes fastest.
Arguments:
- hidden: bfloat16 [36864, 5120], P(('grp', 'tp')), may hold values from -6 to 6
- lengths: int32 [4, 8], P('grp'), may hold values from 1 to 1152, 3686 in all within a row
- kv_weight: bfloat16 [5120, 1024], P('grp', 'tp'), may hold values from -0.078125 to 0.078125
- input_gain: float32 [5120], replicated, may hold values from 0.1 to 1.9
- key_gain: float32 [128], replicated, may hold values from 0.1 to 1.9
Outputs:
- cache_pages: bfloat16 [160, 128, 1024], P(('grp', 'tp'))
Inputs may be any that keep to these rules, and one draw needn't show every extreme that they name: In each group's row the 8 lengths sum to 3686 and the largest equals 1152.
All inputs are finite; a program needn't handle non-finite values.
Results may differ from a plain program's by a relative error of at most 0.0049.
Values may be sent and summed in bfloat16 or wider, within the bound.
No kernel may reach another device: no remote copies, remote signals or barrier semaphores. Data moves between devices by JAX's collectives and lax.ppermute only.
A program may use at most 64 MiB of HBM per device.

v0:
```python
import math

import jax
import jax.numpy as jnp
from jax import lax
from jax.sharding import PartitionSpec as P

HD = 128
KVH = 4
BLK = 128


rope_base = 1000000.0
norm_eps = 1e-06


def normalize(token_rows, input_gain):
    values = token_rows.astype(jnp.float32)
    row_scale = lax.rsqrt(jnp.mean(values * values, axis=-1, keepdims=True) + norm_eps)
    return (values * row_scale * input_gain).astype(jnp.bfloat16)


def finish(projected, positions, valid, key_gain):
    key_width = KVH * HD
    half_dim = HD // 2
    row_count = projected.shape[0]
    key_part = projected[:, :key_width].reshape(row_count, KVH, HD)
    key_scale = lax.rsqrt(jnp.mean(key_part * key_part, axis=-1, keepdims=True) + norm_eps)
    key_part = key_part * key_scale * key_gain
    exponent = jnp.arange(half_dim, dtype=jnp.float32) * (2.0 / HD)
    inverse = jnp.exp(exponent * -math.log(rope_base))
    angles = positions.astype(jnp.float32)[:, None] * inverse[None, :]
    cosine = jnp.cos(angles)[:, None, :]
    sine_part = jnp.sin(angles)[:, None, :]
    lower_half = key_part[..., :half_dim]
    upper_half = key_part[..., half_dim:]
    turned = jnp.concatenate(
        [
            lower_half * cosine - upper_half * sine_part,
            upper_half * cosine + lower_half * sine_part,
        ],
        axis=-1,
    )
    merged = jnp.concatenate(
        [turned.reshape(row_count, key_width), projected[:, key_width:]], axis=-1
    )
    return jnp.where(valid[:, None], merged, 0.0).astype(jnp.bfloat16)


def project(normed, kv_weight):
    all_rows = lax.all_gather(kv_weight, "grp", axis=0, tiled=True)
    return jnp.dot(
        normed,
        lax.all_gather(all_rows, "tp", axis=1, tiled=True),
        preferred_element_type=jnp.float32,
    )


def local(hidden, lengths, kv_weight, input_gain, key_gain):
    tp_count = lax.axis_size("tp")
    my_index = lax.axis_index("tp")
    own_blocks = hidden.shape[0] // BLK
    live_tokens = 2 * tp_count * own_blocks * BLK // 5
    page_count = ((live_tokens + BLK - 1) // BLK + 2 * tp_count - 2) // tp_count
    per_peer = (own_blocks + tp_count - 1) // tp_count
    cache_width = 2 * KVH * HD
    group_len = lengths[0]
    block_counts = (group_len + (BLK - 1)) // BLK
    block_ends = jnp.cumsum(block_counts)
    block_starts = block_ends - block_counts
    offsets = jnp.arange(BLK, dtype=jnp.int32)
    my_start = block_starts[my_index]
    my_count = block_counts[my_index]
    my_length = group_len[my_index]
    outbound = (
        jnp.arange(tp_count, dtype=jnp.int32)[:, None] - my_start
    ) % tp_count + tp_count * jnp.arange(per_peer, dtype=jnp.int32)[None, :]
    outbound = outbound.reshape(-1)
    sending = outbound < my_count
    picked_local = jnp.minimum(outbound, own_blocks - 1)
    page_ranks = tp_count * jnp.arange(page_count, dtype=jnp.int32) + my_index
    anchor = jnp.minimum(
        jnp.sum((block_ends[None, :] <= page_ranks[:, None]).astype(jnp.int32), axis=1),
        tp_count - 1,
    )
    block_index = page_ranks - block_starts[anchor]
    page_live = page_ranks < block_ends[-1]
    chosen = anchor * per_peer + jnp.clip(block_index // tp_count, 0, per_peer - 1)
    projected = project(normalize(hidden, input_gain), kv_weight)
    own_pos = (jnp.arange(own_blocks, dtype=jnp.int32)[:, None] * BLK + offsets[None, :]).reshape(
        -1
    )
    own_cache = finish(projected, own_pos, own_pos < my_length, key_gain).reshape(
        own_blocks, BLK, cache_width
    )
    outgoing = jnp.where(
        sending[:, None, None],
        jnp.take(own_cache, picked_local, axis=0),
        jnp.zeros((), jnp.bfloat16),
    )
    arrived = lax.all_to_all(outgoing, "tp", split_axis=0, concat_axis=0, tiled=True)
    cache_pages = jnp.take(arrived, chosen, axis=0)
    return jnp.where(page_live[:, None, None], cache_pages, jnp.zeros((), jnp.bfloat16))


def solution(mesh):
    placed = (P(("grp", "tp"), None), P("grp", None), P("grp", "tp"), P(), P())
    return jax.shard_map(
        local, mesh=mesh, in_specs=placed, out_specs=P(("grp", "tp"), None, None), check_vma=False
    )
```

profile of v0, /device:TPU:0, one launch (start us, length us, event | category | flops | bytes accessed | tf_op | source)
XLA Modules:
  0.0 291.1 jit_solution(3943506621378698797)
XLA Ops:
  6.5 0.0 all-gather.3.cloned.1.call-start
  6.5 0.7 all-gather.3.cloned.1.call-update
  7.3 0.0 all-gather.5.cloned.1.call-start
  7.3 33.4 %all-gather.3.cloned.1.call-done = bf16[5120,128]{1,0:T(8,128)(2,1)} async-done(((bf16[1280,128]{1,0:T(8,128)(2,1)}), bf16[5120,128]{1,0:T(8,128)(2,1)}) %all-gather.3.cloned.1.call-update) | async-done | bytes 1310736 | tf_op jit(solution)/shard_map/all_gather | solution.py:51
  40.7 0.0 all-gather.5.cloned.1.call-update
  40.8 1.2 constant_dynamic-slice_fusion
  42.0 0.7 and_select_fusion.4
  42.7 0.2 reduce-window.4
  42.9 0.7 bitcast_subtract_fusion.1
  43.5 0.6 dynamic_slice.9
  44.2 0.0 copy-done.4
  44.2 0.6 and_select_fusion.1
  44.8 0.1 add_minimum_fusion
  44.9 0.1 min.50
  45.0 0.1 min.49
  45.0 0.7 dynamic_slice.10
  45.7 0.7 add_compare_fusion
  46.4 0.1 lt.92
  46.5 0.5 compare_and_fusion
  47.0 0.7 fusion.8
  47.8 0.1 convert_bitcast_fusion
  47.8 8.1 %fusion = f32[1152]{0:T(1024)S(1)} fusion(bf16[1152,5120]{1,0:T(8,128)(2,1)} %param.5), kind=kLoop, calls=%fused_computation.5 | loop fusion | flops 17693568 | bytes 11801088 | tf_op jit(solution)/shard_map/reduce_sum | solution.py:19
  55.9 3.4 %multiply_cosine_fusion = (f32[1152,64]{1,0:T(8,128)}, f32[1152,64]{1,0:T(8,128)}) fusion(f32[64]{0:T(128)S(1)} %multiply_exponential_fusion, f32[1152]{0:T(1024)S(1)} %convert_bitcast_fusion), kind=kLoop, calls=%fused_computation.21 | loop fusion | flops 73728 | bytes 594688 | tf_op jit(solution)/shard_map/cos | solution.py:33
  59.4 82.8 %all-gather.5.cloned.1.call-done = bf16[5120,1024]{1,0:T(8,128)(2,1)} async-done(((bf16[5120,128]{1,0:T(8,128)(2,1)}), bf16[5120,1024]{1,0:T(8,128)(2,1)}) %all-gather.5.cloned.1.call-update) | async-done | bytes 10485776 | tf_op jit(solution)/shard_map/all_gather | solution.py:54
  142.2 0.0 copy-done.6
  142.2 17.1 %fusion.3 = f32[1152,1024]{1,0:T(8,128)S(1)} fusion(bf16[5120,1024]{1,0:T(8,128)(2,1)} %all-gather.5.cloned.1.call-done, bf16[1152,5120]{1,0:T(8,128)(2,1)} %param.5, f32[5120]{0:T(1024)S(1)} %copy-done.6, f32[1152]{0:T(1024)S(1)} %add_rsqrt_fusion.1), kind=kOutput, calls=%fused_computation.8 | convolution fusion | flops 12103188480 | bytes 27025920 | tf_op jit(solution)/shard_map/dot_general | solution.py:52
  159.3 1.6 slice.27
  160.9 0.2 slice.30
  161.1 2.6 reshape.377
  163.8 0.0 copy-start.2
  163.8 2.0 multiply_reduce_fusion
  165.8 0.1 add_rsqrt_fusion
  165.9 0.0 copy-start
  165.9 1.5 multiply_multiply_fusion
  167.5 1.8 multiply_subtract_fusion
  169.3 1.7 pad_maximum_fusion
  171.0 1.3 concatenate.12
  172.3 1.7 fusion.7
  174.0 2.8 gather_fusion.1
  176.8 4.7 %select_select_fusion = bf16[16,128,1024]{2,1,0:T(8,128)(2,1)} fusion(bf16[16,128,1024]{2,1,0:T(8,128)(2,1)} %gather_fusion.1, pred[16]{0:T(512)(128)(4,1)S(1)} %copy-done.3, pred[16]{0:T(512)(128)(4,1)S(1)} %lt.92), kind=kLoop, calls=%fused_computation.13 | loop fusion | flops 4194304 | bytes 8388640 | tf_op jit(solution)/shard_map/jit(_where)/select_n | solution.py:96
  181.5 4.7 %all-to-all-start = ((bf16[16,128,1024]{2,1,0:T(8,128)(2,1)}), bf16[16,128,1024]{2,1,0:T(8,128)(2,1)}, u32[]{:S(2)}, u32[]{:S(2)}) async-start(bf16[16,128,1024]{2,1,0:T(8,128)(2,1)} %select_select_fusion), calls=%async_computation | async-start | bytes 8388608 | tf_op jit(solution)/shard_map/all_to_all | solution.py:101
  186.2 0.6 slice.16
  186.8 0.2 convert_reduce_fusion
  187.0 0.6 gather_fusion
  187.7 0.7 compare_and_fusion.1
  188.3 91.8 %all-to-all-done = bf16[16,128,1024]{2,1,0:T(8,128)(2,1)} async-done(((bf16[16,128,1024]{2,1,0:T(8,128)(2,1)}), bf16[16,128,1024]{2,1,0:T(8,128)(2,1)}, u32[]{:S(2)}, u32[]{:S(2)}) %all-to-all-start) | async-done | bytes 4194336 | tf_op jit(solution)/shard_map/all_to_all | solution.py:101
  280.2 2.8 gather_fusion.2
  283.0 1.3 select_select_fusion.1
  (21 shorter events, 0.1 us)
Async XLA Ops:
  6.5 34.2 %all-gather.3.cloned.1.call-start = ((), (), s32[]{:S(2)}) async-start(), calls=%async_computation.1 | async-start | bytes 1638400 | tf_op jit(solution)/shard_map/all_gather | solution.py:51
  7.3 134.9 %all-gather.5.cloned.1.call-start = ((), (), s32[]{:S(2)}) async-start(), calls=%async_computation.2 | async-start | bytes 11796480 | tf_op jit(solution)/shard_map/all_gather | solution.py:54
  42.9 1.3 copy-start.4
  47.8 94.4 %copy-start.6 = (f32[5120]{0:T(1024)S(1)}, f32[5120]{0:T(1024)}, u32[]{:S(2)}) copy-start(f32[5120]{0:T(1024)} %param.8) | copy-start | bytes 61444
  163.8 2.1 copy-start.2
  165.9 1.5 copy-start
  165.9 1.5 copy-start.1
  174.0 2.8 copy-start.3
  181.5 4.7 %copy-start.5 = (s32[8,1]{0,1:T(1,128)S(1)}, s32[8,1]{0,1:T(1,128)}, u32[]{:S(2)}) copy-start(s32[8,1]{0,1:T(1,128)} %copy-done.4) | copy-start | bytes 100
  181.5 98.7 %all-to-all-start = ((bf16[16,128,1024]{2,1,0:T(8,128)(2,1)}), bf16[16,128,1024]{2,1,0:T(8,128)(2,1)}, u32[]{:S(2)}, u32[]{:S(2)}) async-start(bf16[16,128,1024]{2,1,0:T(8,128)(2,1)} %select_select_fusion), calls=%async_computation | async-start | bytes 8388608 | tf_op jit(solution)/shard_map/all_to_all | solution.py:101
Sparse Core Ops, SparseCore 0:
  9.2 31.4 all-gather.2
  42.3 99.8 all-gather.4
where the time goes:
time: 292 us; the launch traced here: 291 us
  waiting for transfers between devices  209 us (72%)
  other arithmetic  31.4 us (11%)
  matrix products  17.1 us (6%)
  local copies, waits for them, and re-layouts  15.4 us (5%)
  between operations  13.6 us (5%)
  starting transfers between devices  4.72 us (2%)
    all_to_all x1, waiting for transfers between devices, local(): lax.all_to_all(outgoing, 'tp', split_axis=0, concat_axis=0, tiled=True)  91.8 us
    all_gather x1, waiting for transfers between devices, project(): lax.all_gather(all_rows, 'tp', axis=1, tiled=True)  82.8 us
    all_gather x1, waiting for transfers between devices, project(): all_rows = lax.all_gather(kv_weight, 'grp', axis=0, tiled=True)  33.4 us
    dot_general x1, matrix products, project(): jnp.dot(normed, lax.all_gather(all_rows, 'tp', axis=1, tiled=True), prefe...  17.1 us
    reduce_sum x1, other arithmetic, normalize(): jnp.mean(values * values, axis=-1, keepdims=True) + norm_eps  8.11 us
  transfers between devices with their start and end apart: 3, of which 3 were waited for; matrix products, arithmetic and copies ran while one was open for 7% of the time, Pallas kernels for 0%

commit v1 on v0

--- a/solution.py
+++ b/solution.py
@@ -1,8 +1,12 @@
+import functools
 import math
 
 import jax
 import jax.numpy as jnp
+import numpy as np
 from jax import lax
+from jax.experimental import pallas as pl
+from jax.experimental.pallas import tpu as pltpu
 from jax.sharding import PartitionSpec as P
 
 HD = 128
@@ -56,12 +60,16 @@
     )
 
 
-def local(hidden, lengths, kv_weight, input_gain, key_gain):
+def pages_per_device(tp_count, own_blocks):
+    live_tokens = 2 * tp_count * own_blocks * BLK // 5
+    return ((live_tokens + BLK - 1) // BLK + 2 * tp_count - 2) // tp_count
+
+
+def general(hidden, lengths, kv_weight, input_gain, key_gain):
     tp_count = lax.axis_size("tp")
     my_index = lax.axis_index("tp")
     own_blocks = hidden.shape[0] // BLK
-    live_tokens = 2 * tp_count * own_blocks * BLK // 5
-    page_count = ((live_tokens + BLK - 1) // BLK + 2 * tp_count - 2) // tp_count
+    page_count = pages_per_device(tp_count, own_blocks)
     per_peer = (own_blocks + tp_count - 1) // tp_count
     cache_width = 2 * KVH * HD
     group_len = lengths[0]
@@ -103,6 +111,463 @@
     return jnp.where(page_live[:, None, None], cache_pages, jnp.zeros((), jnp.bfloat16))
 
 
+def slot_tables(nz):
+    columns, arrival = [], []
+    for z in range(nz):
+        row, came = [z], [(0, 0)]
+        for step in range(1, nz):
+            if z + step < nz:
+                row.append(z + step)
+                came.append((step, 0))
+            if z - step >= 0:
+                row.append(z - step)
+                came.append((step, 1))
+        columns.append(row)
+        arrival.append(came)
+    return columns, arrival
+
+
+def read_table(table, row, column):
+    value = jnp.int32(table[0][column])
+    for index in range(1, len(table)):
+        value = jnp.where(row == index, jnp.int32(table[index][column]), value)
+    return value
+
+
+def line_steps(nz):
+    steps = []
+    for step in range(1, nz):
+        down = [(2 * s + c, 2 * s - 2 + c) for s in range(1, nz) if s - 1 + step < nz for c in range(2)]
+        up = [(2 * s + c, 2 * s + 2 + c) for s in range(nz - 1) if s + 1 - step >= 0 for c in range(2)]
+        steps.append((down, up))
+    return steps
+
+
+def pick_slot(held, slot, nz):
+    z = lax.axis_index("tp") // 2
+    _, arrival = slot_tables(nz)
+    picked = held[arrival[0][slot]]
+    for chip in range(1, nz):
+        if arrival[chip][slot] != arrival[chip - 1][slot]:
+            picked = jnp.where(z >= chip, held[arrival[chip][slot]], picked)
+    return picked
+
+
+flip0 = [(i, i ^ 1) for i in range(4)]
+flip1 = [(i, i ^ 2) for i in range(4)]
+
+
+def sides(shard):
+    return lax.ppermute(shard, "grp", flip0), lax.ppermute(shard, "grp", flip1)
+
+
+def opposite(side_pairs):
+    half = side_pairs[0][0].shape[0] // 2
+    first = jnp.concatenate([side0[:half] for side0, _ in side_pairs])
+    second = jnp.concatenate([side1[half:] for _, side1 in side_pairs])
+    return lax.ppermute(first, "grp", flip1), lax.ppermute(second, "grp", flip0)
+
+
+def scale_kernel(lengths_ref, place_ref, x_ref, out_ref):
+    blocks = (lengths_ref[place_ref[1]] + (BLK - 1)) // BLK
+
+    @pl.when(pl.program_id(0) < blocks)
+    def _():
+        values = x_ref[...].astype(jnp.float32)
+        mean = jnp.mean(values * values, axis=-1, keepdims=True)
+        out_ref[...] = jnp.broadcast_to(lax.rsqrt(mean + norm_eps), out_ref.shape)
+
+
+def row_scales(lengths, place, hidden):
+    rows, width = hidden.shape
+
+    def live(i, lengths_ref, place_ref):
+        return jnp.minimum(i, (lengths_ref[place_ref[1]] + (BLK - 1)) // BLK - 1), 0
+
+    return pl.pallas_call(
+        scale_kernel,
+        grid_spec=pltpu.PrefetchScalarGridSpec(
+            num_scalar_prefetch=2,
+            grid=(rows // BLK,),
+            in_specs=[pl.BlockSpec((BLK, width), live)],
+            out_specs=pl.BlockSpec((BLK, HD), live),
+        ),
+        out_shape=jax.ShapeDtypeStruct((rows, HD), jnp.float32),
+        compiler_params=pltpu.CompilerParams(vmem_limit_bytes=54 << 20),
+        cost_estimate=pl.CostEstimate(
+            flops=3 * rows * width, bytes_accessed=2 * rows * width, transcendentals=0
+        ),
+        name="row_scales",
+    )(lengths, place, hidden)
+
+
+def chip_facts(lengths_ref, chip):
+    first = jnp.int32(0)
+    for index in range(lengths_ref.shape[0]):
+        count = (lengths_ref[index] + (BLK - 1)) // BLK
+        first = first + jnp.where(index < 2 * chip, count, 0)
+    return first, lengths_ref[2 * chip], lengths_ref[2 * chip + 1]
+
+
+def project_kernel(slot_ids, tile, depth, deep, *refs):
+    count = len(slot_ids)
+    lengths_ref, place_ref, own_ref, sib_ref = refs[:4]
+    near = refs[4 : 4 + 3 * count]
+    far = refs[4 + 3 * count : 6 + 3 * count]
+    own_scale, sib_scale, turn_ref, gain_ref, out_ref, over_ref = refs[6 + 3 * count : 12 + 3 * count]
+    x_buf, w_buf, o_buf, x_sem, w_sem, o_sem = refs[12 + 3 * count :]
+    tp_count = lengths_ref.shape[0]
+    ahead = x_buf.shape[0]
+    group, me = place_ref[0], place_ref[1]
+    chip, core = me // 2, me % 2
+    first, length0, length1 = chip_facts(lengths_ref, chip)
+    count0 = (length0 + (BLK - 1)) // BLK
+    own_len = jnp.where(core == 0, length0, length1)
+    sib_len = jnp.where(core == 0, length1, length0)
+    own_count = (own_len + (BLK - 1)) // BLK
+    total = own_count + (sib_len + (BLK - 1)) // BLK
+    tiles = (total + (tile - 1)) // tile
+
+    def within(i):
+        return jnp.where(i < own_count, i, i - own_count)
+
+    def fetch(step, start):
+        slot = lax.rem(step, ahead)
+        for part in range(tile):
+            i = step * tile + part
+            rows = pl.ds(pl.multiple_of(within(i) * BLK, BLK), BLK)
+            target = x_buf.at[slot, pl.ds(part * BLK, BLK)]
+
+            @pl.when(i < own_count)
+            def _():
+                copy = pltpu.make_async_copy(own_ref.at[rows], target, x_sem.at[slot, part])
+                copy.start() if start else copy.wait()
+
+            @pl.when(jnp.logical_and(i >= own_count, i < total))
+            def _():
+                copy = pltpu.make_async_copy(sib_ref.at[rows], target, x_sem.at[slot, part])
+                copy.start() if start else copy.wait()
+
+    copies = []
+    half = depth // 2
+    for index in range(count):
+        parts = [(near[3 * index + flip], flip, 0) for flip in range(3)]
+        parts += [(far[side].at[pl.ds(index * half, half)], 3, side * half) for side in range(2)]
+        for part, (source, flip, offset) in enumerate(parts):
+            rows = pl.ds(pl.multiple_of((group ^ flip) * depth + offset, 16), source.shape[0])
+            copies.append(
+                pltpu.make_async_copy(
+                    source, w_buf.at[rows, pl.ds(index * HD, HD)], w_sem.at[5 * index + part]
+                )
+            )
+    fetch(jnp.int32(0), True)
+    for copy in copies:
+        copy.start()
+    for step in range(1, ahead - 1):
+        fetch(jnp.int32(step), True)
+    for copy in copies:
+        copy.wait()
+
+    columns, _ = slot_tables(tp_count // 2)
+    is_key = [2 * read_table(columns, chip, slot) + core < KVH for slot in slot_ids]
+
+    def send(i, start):
+        second = jnp.where(i < own_count, core, 1 - core)
+        place = within(i) + second * count0
+
+        @pl.when(jnp.logical_and(i < total, place < deep * tp_count))
+        def _():
+            target = out_ref.at[lax.rem(first + place, tp_count), place // tp_count]
+            copy = pltpu.make_async_copy(o_buf.at[i], target, o_sem.at[i])
+            copy.start() if start else copy.wait()
+
+        @pl.when(jnp.logical_and(i < total, place >= deep * tp_count))
+        def _():
+            target = over_ref.at[place - deep * tp_count]
+            copy = pltpu.make_async_copy(o_buf.at[i], target, o_sem.at[i])
+            copy.start() if start else copy.wait()
+
+    def one_tile(step, carry):
+        fetch(step + (ahead - 1), True)
+        fetch(step, False)
+        product = jnp.dot(x_buf[lax.rem(step, ahead)], w_buf[...], preferred_element_type=jnp.float32)
+        blocks = []
+        for part in range(tile):
+            i = jnp.minimum(step * tile + part, total - 1)
+            rows = pl.ds(pl.multiple_of(within(i) * BLK, BLK), BLK)
+            limit = jnp.where(i < own_count, own_len, sib_len) - within(i) * BLK
+            valid = lax.broadcasted_iota(jnp.int32, (BLK, HD), 0) < limit
+            scale = jnp.where(i < own_count, own_scale[rows, :], sib_scale[rows, :])
+            blocks.append((step * tile + part, rows, valid, scale))
+        for index in range(count):
+
+            def scaled(part):
+                cut = product[part * BLK : (part + 1) * BLK, index * HD : (index + 1) * HD]
+                return cut * blocks[part][3]
+
+            def keep(part, values):
+                i, _, valid, _ = blocks[part]
+                o_buf[i, index] = jnp.where(valid, values, 0.0).astype(jnp.bfloat16)
+
+            @pl.when(is_key[index])
+            def _():
+                for part in range(tile):
+                    rows = blocks[part][1]
+                    values = scaled(part)
+                    key_scale = lax.rsqrt(jnp.mean(values * values, axis=-1, keepdims=True) + norm_eps)
+                    keys = values * key_scale * gain_ref[...]
+                    turned = keys * turn_ref[rows, :HD] + pltpu.roll(keys, HD // 2, 1) * turn_ref[rows, HD:]
+                    keep(part, turned)
+
+            @pl.when(jnp.logical_not(is_key[index]))
+            def _():
+                for part in range(tile):
+                    keep(part, scaled(part))
+
+        for part in range(tile):
+            send(step * tile + part, True)
+        return carry
+
+    lax.fori_loop(0, tiles, one_tile, 0)
+
+    def drain(i, carry):
+        send(i, False)
+        return carry
+
+    lax.fori_loop(0, total, drain, 0)
+
+
+def project_slots(slot_ids, lengths, place, own, sibling, near, far, scales, turn, key_gain, deep):
+    rows, width = own.shape
+    tp_count = lengths.shape[0]
+    own_blocks = rows // BLK
+    depth = near[0][0].shape[0]
+    count = len(slot_ids)
+    tile = max(t for t in (1, 2, 3) if own_blocks % t == 0)
+    ahead = 3
+    spare = 2 * own_blocks - deep * tp_count
+    anywhere = pl.BlockSpec(memory_space=pl.ANY)
+    whole = pl.BlockSpec(memory_space=pltpu.VMEM)
+    pieces = [piece for parts in near for piece in parts] + list(far)
+    return pl.pallas_call(
+        functools.partial(project_kernel, slot_ids, tile, depth, deep),
+        in_specs=[pl.BlockSpec(memory_space=pltpu.SMEM)] * 2
+        + [anywhere] * (2 + len(pieces))
+        + [whole] * 4,
+        out_specs=[anywhere, anywhere],
+        out_shape=[
+            jax.ShapeDtypeStruct((tp_count, deep, count, BLK, HD), jnp.bfloat16),
+            jax.ShapeDtypeStruct((max(spare, 1), count, BLK, HD), jnp.bfloat16),
+        ],
+        scratch_shapes=[
+            pltpu.VMEM((ahead, tile * BLK, width), jnp.bfloat16),
+            pltpu.VMEM((width, count * HD), jnp.bfloat16),
+            pltpu.VMEM((2 * own_blocks + tile, count, BLK, HD), jnp.bfloat16),
+            pltpu.SemaphoreType.DMA((ahead, tile)),
+            pltpu.SemaphoreType.DMA((5 * count,)),
+            pltpu.SemaphoreType.DMA((2 * own_blocks,)),
+        ],
+        compiler_params=pltpu.CompilerParams(vmem_limit_bytes=54 << 20),
+        cost_estimate=pl.CostEstimate(
+            flops=4 * rows * width * count * HD,
+            bytes_accessed=4 * rows * width + 2 * width * count * HD,
+            transcendentals=0,
+        ),
+        name="project_slots",
+    )(lengths, place, own, sibling, *pieces, scales[0], scales[1], turn, key_gain)
+
+
+def page_source(lengths_ref, place_ref, page):
+    tp_count = lengths_ref.shape[0]
+    rank = page * tp_count + place_ref[1]
+    end, chip, first = jnp.int32(0), jnp.int32(0), jnp.int32(0)
+    for index in range(tp_count):
+        end = end + (lengths_ref[index] + (BLK - 1)) // BLK
+        if index % 2 == 1 and index + 1 < tp_count:
+            passed = end <= rank
+            chip = jnp.where(passed, index // 2 + 1, chip)
+            first = jnp.where(passed, end, first)
+    return rank < end, chip, rank - first
+
+
+def assemble_kernel(groups, tp_count, deep, lengths_ref, place_ref, *refs):
+    out_ref = refs[-1]
+    live, chip, within = page_source(lengths_ref, place_ref, pl.program_id(0))
+    columns, _ = slot_tables(tp_count // 2)
+    over = within >= deep * tp_count
+    spilled = len(refs) > 2 * len(groups) + 1
+    per_group = 4 if spilled else 2
+
+    @pl.when(live)
+    def _():
+        for place, slot_ids in enumerate(groups):
+            for core in range(2):
+                for index, slot in enumerate(slot_ids):
+                    column = 2 * read_table(columns, chip, slot) + core
+                    target = pl.ds(pl.multiple_of(column * HD, HD), HD)
+                    block = refs[per_group * place + core][0, 0, index]
+                    if spilled:
+                        block = jnp.where(over, refs[per_group * place + 2 + core][0, 0, index], block)
+                    out_ref[0, :, target] = block
+
+    @pl.when(jnp.logical_not(live))
+    def _():
+        out_ref[...] = jnp.zeros_like(out_ref)
+
+
+def assemble(groups, lengths, place, arrived, spilled, page_count, deep):
+    tp_count = lengths.shape[0]
+    operands, specs = [], []
+
+    def spec_for(count, core, spill):
+        def index_map(page, lengths_ref, place_ref):
+            live, chip, within = page_source(lengths_ref, place_ref, page)
+            if spill:
+                position = jnp.clip(within - deep * tp_count, 0, spill - 1)
+            else:
+                position = jnp.clip(within // tp_count, 0, deep - 1)
+            return 2 * chip + core, position, 0, 0, 0
+
+        return pl.BlockSpec((1, 1, count, BLK, HD), index_map)
+
+    for place_of, slot_ids in enumerate(groups):
+        for core in range(2):
+            operands.append(arrived[place_of])
+            specs.append(spec_for(len(slot_ids), core, 0))
+        if spilled is not None:
+            for core in range(2):
+                operands.append(spilled[place_of])
+                specs.append(spec_for(len(slot_ids), core, spilled[place_of].shape[1]))
+    return pl.pallas_call(
+        functools.partial(assemble_kernel, groups, tp_count, deep),
+        grid_spec=pltpu.PrefetchScalarGridSpec(
+            num_scalar_prefetch=2,
+            grid=(page_count,),
+            in_specs=specs,
+            out_specs=pl.BlockSpec((1, BLK, 2 * KVH * HD), lambda page, *_: (page, 0, 0)),
+        ),
+        out_shape=jax.ShapeDtypeStruct((page_count, BLK, 2 * KVH * HD), jnp.bfloat16),
+        compiler_params=pltpu.CompilerParams(vmem_limit_bytes=54 << 20),
+        name="assemble",
+    )(lengths, place, *operands)
+
+
+def rope_table(rows):
+    exponent = jnp.arange(HD // 2, dtype=jnp.float32) * (2.0 / HD)
+    inverse = jnp.exp(exponent * -math.log(rope_base))
+    angles = jnp.arange(rows, dtype=jnp.float32)[:, None] * inverse[None, :]
+    cosine, sine_part = jnp.cos(angles), jnp.sin(angles)
+    return jnp.concatenate([cosine, cosine, -sine_part, sine_part], axis=1)
+
+
+def exchange(sent):
+    return lax.all_to_all(sent, "tp", split_axis=0, concat_axis=0, tiled=True)
+
+
+def paired(hidden, lengths, kv_weight, input_gain, key_gain):
+    tp_count = lax.axis_size("tp")
+    nz = tp_count // 2
+    group, me = lax.axis_index("grp"), lax.axis_index("tp")
+    rows = hidden.shape[0]
+    own_blocks = rows // BLK
+    depth = kv_weight.shape[0]
+    deep = 2 * own_blocks // tp_count
+    page_count = pages_per_device(tp_count, own_blocks)
+    group_len = lengths[0]
+    place = jnp.stack([group, me]).astype(jnp.int32)
+    swap = [(i, i ^ 1) for i in range(tp_count)]
+
+    own_gain = lax.dynamic_slice(input_gain, (group * depth,), (depth,))
+    shard = (kv_weight.astype(jnp.float32) * own_gain[:, None]).astype(jnp.bfloat16)
+    sibling = lax.ppermute(hidden, "tp", swap)
+    gain = key_gain.reshape(1, HD)
+
+    steps = line_steps(nz)
+    held, slots = {(0, 0): shard}, [shard]
+    groups = [tuple(range(start, min(start + 2, nz))) for start in range(0, nz, 2)]
+    arrived, over = [], []
+    below, above = shard, shard
+    turn, scale, other_scale = None, None, None
+    sent = None
+    step = 0
+    for slot_ids in groups:
+        rounds = [slot_ids] if slots[slot_ids[0] :] and len(slots) > slot_ids[-1] else [(slot,) for slot in slot_ids]
+        near = []
+        for part in range(len(rounds) + 1):
+            moved, beside = (), {}
+            if part < len(rounds):
+                crossed = sides(jnp.concatenate([slots[slot] for slot in rounds[part]]))
+            else:
+                if step >= 2 and other_scale is None:
+                    other_scale = beside["other"] = lax.ppermute(scale, "tp", swap)
+                crossed = opposite([pair[1:] for pair in near])
+            if step < len(steps):
+                down, up = steps[step]
+                step += 1
+                moved = lax.ppermute(above, "tp", down), lax.ppermute(below, "tp", up)
+            if scale is None:
+                scale = beside["scale"] = row_scales(group_len, place, hidden)
+            elif turn is None:
+                turn = beside["turn"] = rope_table(rows)
+                beside["sibling"] = sibling
+            elif sent is not None:
+                beside["sent"] = sent
+            moved, crossed, beside = lax.optimization_barrier((moved, crossed, beside))
+            turn, scale = beside.get("turn", turn), beside.get("scale", scale)
+            sibling, other_scale = beside.get("sibling", sibling), beside.get("other", other_scale)
+            if "sent" in beside:
+                arrived.append(exchange(beside["sent"]))
+                sent = None
+            if moved:
+                above, below = moved
+                held[(step, 0)], held[(step, 1)] = moved
+            if part < len(rounds):
+                for index, slot in enumerate(rounds[part]):
+                    cut = slice(index * depth, (index + 1) * depth)
+                    near.append((slots[slot], crossed[0][cut], crossed[1][cut]))
+            while len(slots) < nz and all(
+                arrival[len(slots)] in held for arrival in slot_tables(nz)[1]
+            ):
+                slots.append(pick_slot(held, len(slots), nz))
+        sent, rest = project_slots(
+            slot_ids, group_len, place, hidden, sibling, near, crossed, (scale, other_scale), turn, gain, deep
+        )
+        over.append(rest)
+    arrived.append(exchange(sent))
+
+    def plain(operands):
+        return assemble(groups, group_len, place, operands[0], None, page_count, deep)
+
+    if 2 * own_blocks == deep * tp_count:
+        return plain((arrived, over))
+
+    def spilling(operands):
+        spilled = []
+        for rest in operands[1]:
+            got = [rest]
+            for flip in range(1, tp_count):
+                got.append(lax.ppermute(rest, "tp", [(i, i ^ flip) for i in range(tp_count)]))
+            spilled.append(jnp.take(jnp.stack(got), jnp.arange(tp_count) ^ me, axis=0))
+        return assemble(groups, group_len, place, operands[0], spilled, page_count, deep)
+
+    counts = (group_len + (BLK - 1)) // BLK
+    most = jnp.max(counts[0::2] + counts[1::2])
+    return lax.cond(most > deep * tp_count, spilling, plain, (arrived, over))
+
+
+def local(hidden, lengths, kv_weight, input_gain, key_gain):
+    tp_count = lax.axis_size("tp")
+    fits = (
+        lax.axis_size("grp") == 4
+        and tp_count & (tp_count - 1) == 0
+        and kv_weight.shape[1] == HD
+        and kv_weight.shape[0] % 256 == 0
+        and 2 * (hidden.shape[0] // BLK) >= tp_count
+    )
+    chosen = paired if fits else general
+    return chosen(hidden, lengths, kv_weight, input_gain, key_gain)
+
+
 def solution(mesh):
     placed = (P(("grp", "tp"), None), P("grp", None), P("grp", "tp"), P(), P())
     return jax.shard_map(

time: 292 us -> 134 us (0.46)
  waiting for transfers between devices: 209 us -> 50 us
  Pallas kernels: 0 us -> 39.7 us
  starting transfers between devices: 4.72 us -> 28 us
  other arithmetic: 31.4 us -> 8.53 us
  matrix products: 17.1 us -> 0 us
  between operations: 13.6 us -> 1.03 us
  local copies, waits for them, and re-layouts: 15.4 us -> 6.08 us
    all_gather x2 -> x0, waiting for transfers between devices: 116 us -> none  [the longest x1 82.8 us: project(): lax.all_gather(all_rows, 'tp', axis=1, tiled=True)]
    all_to_all x1 -> x2, waiting for transfers between devices: 91.8 us -> 26.5 us  [exchange(): return lax.all_to_all(sent, 'tp', split_axis=0, concat_axis=0, tiled=True)]
    pallas_call x0 -> x4, Pallas kernels: none -> 39.7 us  [the longest x2 28.3 us: project_slots(): pl.pallas_call(functools.partial(project_kernel, slot_ids, tile, depth, d...]
    ppermute x0 -> x18, waiting for transfers between devices: none -> 23.5 us  [the longest x2 10.7 us: opposite(): lax.ppermute(second, 'grp', flip0)]
    ppermute x0 -> x18, starting transfers between devices: none -> 20.9 us  [the longest x6 11.8 us: paired(): moved = (lax.ppermute(above, 'tp', down), lax.ppermute(below, 'tp', up))]
    dot_general x1 -> x0, matrix products: 17.1 us -> none  [project(): jnp.dot(normed, lax.all_gather(all_rows, 'tp', axis=1, tiled=True), prefe...]
    reduce_sum x3 -> x0, other arithmetic: 10.3 us -> none  [the longest x1 8.11 us: normalize(): jnp.mean(values * values, axis=-1, keepdims=True) + norm_eps]
    gather x3 -> x0, local copies, waits for them, and re-layouts: 6.26 us -> none  [the longest x1 2.82 us: local(): cache_pages = jnp.take(arrived, chosen, axis=0)]
  transfers between devices with their start and end apart: 3 -> 20, of which waited for: 3 -> 10; matrix products, arithmetic and copies ran while one was open for 7% -> 9% of each run, Pallas kernels for 0% -> 29%
where the time goes in v1:
time: 134 us
  waiting for transfers between devices  50 us (37%)
  Pallas kernels  39.7 us (30%)
  starting transfers between devices  28 us (21%)
  other arithmetic  8.53 us (6%)
  local copies, waits for them, and re-layouts  6.08 us (5%)
    pallas_call x2, Pallas kernels, project_slots(): pl.pallas_call(functools.partial(project_kernel, slot_ids, tile, depth, d...  28.3 us
    all_to_all x2, waiting for transfers between devices, exchange(): return lax.all_to_all(sent, 'tp', split_axis=0, concat_axis=0, tiled=True)  26.5 us
    ppermute x6, starting transfers between devices, paired(): moved = (lax.ppermute(above, 'tp', down), lax.ppermute(below, 'tp', up))  11.8 us
    ppermute x2, waiting for transfers between devices, opposite(): lax.ppermute(second, 'grp', flip0)  10.7 us
    pallas_call x1, Pallas kernels, row_scales(): pl.pallas_call(scale_kernel, grid_spec=pltpu.PrefetchScalarGridSpec(num_s...  10.1 us
    ppermute x6, waiting for transfers between devices, paired(): moved = (lax.ppermute(above, 'tp', down), lax.ppermute(below, 'tp', up))  7.71 us
    all_to_all x2, starting transfers between devices, exchange(): return lax.all_to_all(sent, 'tp', split_axis=0, concat_axis=0, tiled=True)  7.13 us
    ppermute x3, starting transfers between devices, sides(): lax.ppermute(shard, 'grp', flip1)  3.32 us
  transfers between devices with their start and end apart: 20, of which 10 were waited for; matrix products, arithmetic and copies ran while one was open for 9% of the time, Pallas kernels for 29%

profile of v1, /device:TPU:0, one launch (start us, length us, event | category | flops | bytes accessed | tf_op | source)
XLA Modules:
  0.0 133.6 jit_solution(7884316600058377447)
XLA Ops:
  0.0 0.5 collective-permute-start.22
  0.5 0.8 dynamic_slice.3
  1.2 1.2 multiply_convert_fusion.refs_4_
  2.5 1.3 collective-permute-start.14
  3.8 5.1 %collective-permute-start.15 = (bf16[1280,128]{1,0:T(8,128)(2,1)S(1)}, bf16[1280,128]{1,0:T(8,128)(2,1)S(1)}, u32[]{:S(2)}, u32[]{:S(2)}) collective-permute-start(bf16[1280,128]{1,0:T(8,128)(2,1)S(1)} %multiply_convert_fusion.refs_4_), channel_id=1, source_target_pairs={{0,2},{1,3},{2,4},{3,5},{4,6},{5,7},{8,10},{9,11},{10,12},{11,13},... | collective-permute-start | bytes 983048 | tf_op jit(solution)/shard_map/ppermute | solution.py:507
  8.9 2.0 %collective-permute-start.16 = (bf16[1280,128]{1,0:T(8,128)(2,1)S(1)}, bf16[1280,128]{1,0:T(8,128)(2,1)S(1)}, u32[]{:S(2)}, u32[]{:S(2)}) collective-permute-start(bf16[1280,128]{1,0:T(8,128)(2,1)S(1)} %multiply_convert_fusion.refs_4_), channel_id=1, source_target_pairs={{0,8},{8,0},{16,24},{24,16},{1,9},{9,1},{17,25},{25,17},{2,10},{10... | collective-permute-start | bytes 983048 | tf_op jit(solution)/shard_map/ppermute | solution.py:161
  10.9 1.5 %collective-permute-start.17 = (bf16[1280,128]{1,0:T(8,128)(2,1)S(1)}, bf16[1280,128]{1,0:T(8,128)(2,1)S(1)}, u32[]{:S(2)}, u32[]{:S(2)}) collective-permute-start(bf16[1280,128]{1,0:T(8,128)(2,1)S(1)} %multiply_convert_fusion.refs_4_), channel_id=1, source_target_pairs={{0,16},{8,24},{16,0},{24,8},{1,17},{9,25},{17,1},{25,9},{2,18},{10... | collective-permute-start | bytes 983048 | tf_op jit(solution)/shard_map/ppermute | solution.py:161
  12.4 0.1 pad_add_fusion.place_ref.refs_1_
  12.5 10.1 %row_scales.1.refs_12_ = f32[1152,128]{1,0:T(8,128)} custom-call(s32[8]{0:T(128)} %bitcast.37, s32[2]{0:T(128)S(1)} %pad_add_fusion.place_ref.refs_1_, bf16[1152,5120]{1,0:T(8,128)(2,1)} %refs_2_.3), custom_call_target="tpu_custom_call" | custom-call | flops 17694720 | bytes 11796480 | tf_op jit(solution)/shard_map/row_scales/pallas_call | solution.py:187
  22.7 0.1 collective-permute-start.20
  22.9 1.4 %collective-permute-start.19 = (bf16[1280,128]{1,0:T(8,128)(2,1)S(1)}, bf16[1280,128]{1,0:T(8,128)(2,1)}, u32[]{:S(2)}, u32[]{:S(2)}) collective-permute-start(bf16[1280,128]{1,0:T(8,128)(2,1)S(1)} %collective-permute-done.15), channel_id=1, source_target_pairs={{2,4},{3,5},{4,6},{5,7},{10,12},{11,13},{12,14},{13,15},{18,20},{1... | collective-permute-start | bytes 983048 | tf_op jit(solution)/shard_map/ppermute | solution.py:507
  24.3 1.3 collective-permute-start.18
  25.6 2.2 %fusion.1 = (f32[1152,64]{1,0:T(8,128)S(1)}, f32[1152,64]{1,0:T(8,128)S(1)}, f32[1152,64]{1,0:T(8,128)S(1)}) fusion(f32[64]{0:T(128)S(1)} %multiply_exponential_fusion), kind=kLoop, calls=%fused_computation.28 | loop fusion | flops 147456 | bytes 884992 | tf_op jit(solution)/shard_map/cos | solution.py:459
  27.8 1.6 %pad_maximum_fusion.refs_14_ = f32[1152,256]{1,0:T(8,128)} fusion(f32[1152,64]{1,0:T(8,128)S(1)} %get-tuple-element.109, f32[1152,64]{1,0:T(8,128)S(1)} %get-tuple-element.108, f32[1152,64]{1,0:T(8,128)S(1)} %get-tuple-element.107), kind=kLoop, calls=%fused_computation.23 | loop fusion | flops 884736 | bytes 2064384 | tf_op jit(solution)/shard_map/concatenate | solution.py:460
  29.4 1.2 collective-permute-done.20.refs_8_
  30.6 1.4 %collective-permute-done.21.refs_9_ = bf16[1280,128]{1,0:T(8,128)(2,1)S(1)} collective-permute-done((bf16[1280,128]{1,0:T(8,128)(2,1)S(1)}, bf16[1280,128]{1,0:T(8,128)(2,1)S(1)}, u32[]{:S(2)}, u32[]{:S(2)}) %collective-permute-start.21) | collective-permute-done | bytes 327712 | tf_op jit(solution)/shard_map/ppermute | solution.py:161
  32.0 5.8 %collective-permute-done.18 = bf16[1280,128]{1,0:T(8,128)(2,1)} collective-permute-done((bf16[1280,128]{1,0:T(8,128)(2,1)S(1)}, bf16[1280,128]{1,0:T(8,128)(2,1)}, u32[]{:S(2)}, u32[]{:S(2)}) %collective-permute-start.18) | collective-permute-done | bytes 327712 | tf_op jit(solution)/shard_map/ppermute | solution.py:507
  37.9 0.8 pad_maximum_fusion.3
  38.7 1.7 %collective-permute-start.26 = (bf16[1280,128]{1,0:T(8,128)(2,1)}, bf16[1280,128]{1,0:T(8,128)(2,1)S(1)}, u32[]{:S(2)}, u32[]{:S(2)}) collective-permute-start(bf16[1280,128]{1,0:T(8,128)(2,1)} %pad_maximum_fusion.3), channel_id=1, source_target_pairs={{0,8},{8,0},{16,24},{24,16},{1,9},{9,1},{17,25},{25,17},{2,10},{10... | collective-permute-start | bytes 983048 | tf_op jit(solution)/shard_map/ppermute | solution.py:168
  40.3 0.8 pad_maximum_fusion.2
  41.1 0.3 collective-permute-start.25
  41.4 1.3 collective-permute-start.23
  42.7 1.4 %collective-permute-start.24 = (bf16[1280,128]{1,0:T(8,128)(2,1)}, bf16[1280,128]{1,0:T(8,128)(2,1)}, u32[]{:S(2)}, u32[]{:S(2)}) collective-permute-start(bf16[1280,128]{1,0:T(8,128)(2,1)} %collective-permute-done.19), channel_id=1, source_target_pairs={{4,6},{5,7},{12,14},{13,15},{20,22},{21,23},{28,30},{29,31}} | collective-permute-start | bytes 983048 | tf_op jit(solution)/shard_map/ppermute | solution.py:507
  44.1 3.8 %collective-permute-done.26.refs_11_ = bf16[1280,128]{1,0:T(8,128)(2,1)S(1)} collective-permute-done((bf16[1280,128]{1,0:T(8,128)(2,1)}, bf16[1280,128]{1,0:T(8,128)(2,1)S(1)}, u32[]{:S(2)}, u32[]{:S(2)}) %collective-permute-start.26) | collective-permute-done | bytes 327712 | tf_op jit(solution)/shard_map/ppermute | solution.py:168
  47.9 2.3 %collective-permute-done.25.refs_10_ = bf16[1280,128]{1,0:T(8,128)(2,1)S(1)} collective-permute-done((bf16[1280,128]{1,0:T(8,128)(2,1)}, bf16[1280,128]{1,0:T(8,128)(2,1)S(1)}, u32[]{:S(2)}, u32[]{:S(2)}) %collective-permute-start.25) | collective-permute-done | bytes 327712 | tf_op jit(solution)/shard_map/ppermute | solution.py:168
  50.2 1.9 %collective-permute-done.23 = bf16[1280,128]{1,0:T(8,128)(2,1)S(1)} collective-permute-done((bf16[1280,128]{1,0:T(8,128)(2,1)}, bf16[1280,128]{1,0:T(8,128)(2,1)S(1)}, u32[]{:S(2)}, u32[]{:S(2)}) %collective-permute-start.23) | collective-permute-done | bytes 327712 | tf_op jit(solution)/shard_map/ppermute | solution.py:507
  52.1 1.2 select_select_fusion.1
  53.3 0.3 collective-permute-start.28
  53.7 1.7 %collective-permute-start.29 = (bf16[2560,128]{1,0:T(8,128)(2,1)S(1)}, bf16[2560,128]{1,0:T(8,128)(2,1)}, u32[]{:S(2)}, u32[]{:S(2)}) collective-permute-start(bf16[2560,128]{1,0:T(8,128)(2,1)S(1)} %pad_maximum_fusion.1), channel_id=1, source_target_pairs={{0,16},{8,24},{16,0},{24,8},{1,17},{9,25},{17,1},{25,9},{2,18},{10... | collective-permute-start | bytes 1966088 | tf_op jit(solution)/shard_map/ppermute | solution.py:161
  55.4 15.3 %project_slots.2 = (bf16[8,2,2,128,128]{4,3,2,1,0:T(8,128)(2,1)}, bf16[2,2,128,128]{3,2,1,0:T(8,128)(2,1)}) custom-call(s32[8]{0:T(128)S(1)} %bitcast.38, s32[2]{0:T(128)S(1)} %pad_add_fusion.place_ref.refs_1_, bf16[1152,5120]{1,0:T(8,128)(2,1)} %refs_2_.3, bf16[1152,5120]{1,0:T(8,128)(2,1)} %collective-permute-done.22.refs_3_, bf16[1280,128]{1,0:T(8,128)(2,1)} %copy-done.5, ...), custom_call_target="tpu_custom_call" | custom-call | flops 6039797760 | bytes 26214400 | tf_op jit(solution)/shard_map/project_slots/pallas_call | solution.py:352
  70.8 3.6 %all-to-all-start = ((bf16[8,2,2,128,128]{4,3,2,1,0:T(8,128)(2,1)}), bf16[8,2,2,128,128]{4,3,2,1,0:T(8,128)(2,1)S(1)}, u32[]{:S(2)}, u32[]{:S(2)}) async-start(bf16[8,2,2,128,128]{4,3,2,1,0:T(8,128)(2,1)} %get-tuple-element.84), calls=%async_computation | async-start | bytes 2097152 | tf_op jit(solution)/shard_map/all_to_all | solution.py:464
  74.4 1.0 fusion.3
  75.6 0.9 collective-permute-start.30
  76.5 2.2 %fusion.5 = (bf16[1280,128]{1,0:T(8,128)(2,1)}, bf16[1280,128]{1,0:T(8,128)(2,1)}, bf16[1280,128]{1,0:T(8,128)(2,1)}, bf16[1280,128]{1,0:T(8,128)(2,1)}) fusion(bf16[2560,128]{1,0:T(8,128)(2,1)} %collective-permute-done.29, bf16[2560,128]{1,0:T(8,128)(2,1)S(1)} %collective-permute-done.28), kind=kLoop, calls=%fused_computation.46 | loop fusion | bytes 2621440 | tf_op jit(solution)/shard_map/slice | solution.py:527
  78.7 6.9 %collective-permute-done.31.refs_11_ = bf16[1280,128]{1,0:T(8,128)(2,1)S(1)} collective-permute-done((bf16[1280,128]{1,0:T(8,128)(2,1)S(1)}, bf16[1280,128]{1,0:T(8,128)(2,1)S(1)}, u32[]{:S(2)}, u32[]{:S(2)}) %collective-permute-start.31) | collective-permute-done | bytes 327712 | tf_op jit(solution)/shard_map/ppermute | solution.py:168
  85.6 0.1 collective-permute-done.30.refs_10_
  85.7 0.6 copy-done.13
  86.3 0.1 copy-done.14
  86.4 12.9 %project_slots.3 = (bf16[8,2,2,128,128]{4,3,2,1,0:T(8,128)(2,1)}, bf16[2,2,128,128]{3,2,1,0:T(8,128)(2,1)}) custom-call(s32[8]{0:T(128)S(1)} %bitcast.39, s32[2]{0:T(128)S(1)} %pad_add_fusion.place_ref.refs_1_, bf16[1152,5120]{1,0:T(8,128)(2,1)} %refs_2_.3, bf16[1152,5120]{1,0:T(8,128)(2,1)} %collective-permute-done.22.refs_3_, bf16[1280,128]{1,0:T(8,128)(2,1)} %copy-done.1, ...), custom_call_target="tpu_custom_call" | custom-call | flops 6039797760 | bytes 26214400 | tf_op jit(solution)/shard_map/project_slots/pallas_call | solution.py:352
  99.4 1.5 %all-to-all-done = bf16[8,2,2,128,128]{4,3,2,1,0:T(8,128)(2,1)S(1)} async-done(((bf16[8,2,2,128,128]{4,3,2,1,0:T(8,128)(2,1)}), bf16[8,2,2,128,128]{4,3,2,1,0:T(8,128)(2,1)S(1)}, u32[]{:S(2)}, u32[]{:S(2)}) %all-to-all-start) | async-done | bytes 1048608 | tf_op jit(solution)/shard_map/all_to_all | solution.py:464
  100.9 3.6 %all-to-all-start.1 = ((bf16[8,2,2,128,128]{4,3,2,1,0:T(8,128)(2,1)}), bf16[8,2,2,128,128]{4,3,2,1,0:T(8,128)(2,1)S(1)}, u32[]{:S(2)}, u32[]{:S(2)}) async-start(bf16[8,2,2,128,128]{4,3,2,1,0:T(8,128)(2,1)} %get-tuple-element.89), calls=%async_computation.1 | async-start | bytes 2097152 | tf_op jit(solution)/shard_map/all_to_all | solution.py:464
  104.5 0.1 slice.46
  104.6 0.1 slice.47
  104.7 0.6 add_reduce_fusion
  106.0 25.0 %all-to-all-done.1 = bf16[8,2,2,128,128]{4,3,2,1,0:T(8,128)(2,1)S(1)} async-done(((bf16[8,2,2,128,128]{4,3,2,1,0:T(8,128)(2,1)}), bf16[8,2,2,128,128]{4,3,2,1,0:T(8,128)(2,1)S(1)}, u32[]{:S(2)}, u32[]{:S(2)}) %all-to-all-start.1) | async-done | bytes 1048608 | tf_op jit(solution)/shard_map/all_to_all | solution.py:464
  131.0 1.5 %conditional.1 = (bf16[5,128,1024]{2,1,0:T(8,128)(2,1)S(1)}) conditional(s32[]{:T(128)} %convert_element_type.9, (s32[8]{0:T(128)S(1)}, s32[2]{0:T(128)S(1)}, bf16[8,2,2,128,128]{4,3,2,1,0:T(8,128)(2,1)S(1)}, bf16[8,2,2,128,128]{4,3,2,1,0:T(8,128)(2,1)S(1)}) %tuple.42, (bf16[2,2,128,128]{3,2,1,0:T(8,128)(2,1)}, s32[]{:T(128)}, ...), branch_computations={%region_1.2_spmd, %region_2.4_spmd} | conditional | flops 1049688 | bytes 19927760 | solution.py:555
  131.0 1.3 assemble.2
  132.5 1.0 copy-done.6
  (53 shorter events, 0.4 us)
Async XLA Ops:
  0.0 37.9 %collective-permute-start.22 = (bf16[1152,5120]{1,0:T(8,128)(2,1)}, bf16[1152,5120]{1,0:T(8,128)(2,1)}, u32[]{:S(2)}, u32[]{:S(2)}) collective-permute-start(bf16[1152,5120]{1,0:T(8,128)(2,1)} %refs_2_.3), channel_id=1, source_target_pairs={{0,1},{1,0},{2,3},{3,2},{4,5},{5,4},{6,7},{7,6},{8,9},{9,8},{10,11... | collective-permute-start | bytes 35389448 | tf_op jit(solution)/shard_map/ppermute | solution.py:482
  2.4 20.1 %copy-start.5 = (bf16[1280,128]{1,0:T(8,128)(2,1)}, bf16[1280,128]{1,0:T(8,128)(2,1)S(1)}, u32[]{:S(2)}) copy-start(bf16[1280,128]{1,0:T(8,128)(2,1)S(1)} %multiply_convert_fusion.refs_4_) | copy-start | bytes 983044
  2.5 20.1 %collective-permute-start.14 = (bf16[1280,128]{1,0:T(8,128)(2,1)S(1)}, bf16[1280,128]{1,0:T(8,128)(2,1)S(1)}, u32[]{:S(2)}, u32[]{:S(2)}) collective-permute-start(bf16[1280,128]{1,0:T(8,128)(2,1)S(1)} %multiply_convert_fusion.refs_4_), channel_id=1, source_target_pairs={{2,0},{3,1},{4,2},{5,3},{6,4},{7,5},{10,8},{11,9},{12,10},{13,11},... | collective-permute-start | bytes 983048 | tf_op jit(solution)/shard_map/ppermute | solution.py:507
  3.8 18.8 %collective-permute-start.15 = (bf16[1280,128]{1,0:T(8,128)(2,1)S(1)}, bf16[1280,128]{1,0:T(8,128)(2,1)S(1)}, u32[]{:S(2)}, u32[]{:S(2)}) collective-permute-start(bf16[1280,128]{1,0:T(8,128)(2,1)S(1)} %multiply_convert_fusion.refs_4_), channel_id=1, source_target_pairs={{0,2},{1,3},{2,4},{3,5},{4,6},{5,7},{8,10},{9,11},{10,12},{11,13},... | collective-permute-start | bytes 983048 | tf_op jit(solution)/shard_map/ppermute | solution.py:507
  8.9 13.7 %collective-permute-start.16 = (bf16[1280,128]{1,0:T(8,128)(2,1)S(1)}, bf16[1280,128]{1,0:T(8,128)(2,1)S(1)}, u32[]{:S(2)}, u32[]{:S(2)}) collective-permute-start(bf16[1280,128]{1,0:T(8,128)(2,1)S(1)} %multiply_convert_fusion.refs_4_), channel_id=1, source_target_pairs={{0,8},{8,0},{16,24},{24,16},{1,9},{9,1},{17,25},{25,17},{2,10},{10... | collective-permute-start | bytes 983048 | tf_op jit(solution)/shard_map/ppermute | solution.py:161
  10.9 11.7 %collective-permute-start.17 = (bf16[1280,128]{1,0:T(8,128)(2,1)S(1)}, bf16[1280,128]{1,0:T(8,128)(2,1)S(1)}, u32[]{:S(2)}, u32[]{:S(2)}) collective-permute-start(bf16[1280,128]{1,0:T(8,128)(2,1)S(1)} %multiply_convert_fusion.refs_4_), channel_id=1, source_target_pairs={{0,16},{8,24},{16,0},{24,8},{1,17},{9,25},{17,1},{25,9},{2,18},{10... | collective-permute-start | bytes 983048 | tf_op jit(solution)/shard_map/ppermute | solution.py:161
  22.6 6.7 %copy-start.7 = (bf16[1280,128]{1,0:T(8,128)(2,1)}, bf16[1280,128]{1,0:T(8,128)(2,1)S(1)}, u32[]{:S(2)}) copy-start(bf16[1280,128]{1,0:T(8,128)(2,1)S(1)} %collective-permute-done.16.refs_5_) | copy-start | bytes 983044
  22.6 6.7 %copy-start.8 = (bf16[1280,128]{1,0:T(8,128)(2,1)}, bf16[1280,128]{1,0:T(8,128)(2,1)S(1)}, u32[]{:S(2)}) copy-start(bf16[1280,128]{1,0:T(8,128)(2,1)S(1)} %collective-permute-done.17.refs_6_) | copy-start | bytes 983044
  22.7 6.6 %copy-start.4 = (bf16[1280,128]{1,0:T(8,128)(2,1)}, bf16[1280,128]{1,0:T(8,128)(2,1)S(1)}, u32[]{:S(2)}) copy-start(bf16[1280,128]{1,0:T(8,128)(2,1)S(1)} %broadcast_select_fusion.2.refs_7_) | copy-start | bytes 983044
  22.7 7.9 %collective-permute-start.20 = (bf16[1280,128]{1,0:T(8,128)(2,1)S(1)}, bf16[1280,128]{1,0:T(8,128)(2,1)S(1)}, u32[]{:S(2)}, u32[]{:S(2)}) collective-permute-start(bf16[1280,128]{1,0:T(8,128)(2,1)S(1)} %broadcast_select_fusion.2.refs_7_), channel_id=1, source_target_pairs={{0,8},{8,0},{16,24},{24,16},{1,9},{9,1},{17,25},{25,17},{2,10},{10... | collective-permute-start | bytes 983048 | tf_op jit(solution)/shard_map/ppermute | solution.py:161
  22.8 9.3 %collective-permute-start.21 = (bf16[1280,128]{1,0:T(8,128)(2,1)S(1)}, bf16[1280,128]{1,0:T(8,128)(2,1)S(1)}, u32[]{:S(2)}, u32[]{:S(2)}) collective-permute-start(bf16[1280,128]{1,0:T(8,128)(2,1)S(1)} %broadcast_select_fusion.2.refs_7_), channel_id=1, source_target_pairs={{0,16},{8,24},{16,0},{24,8},{1,17},{9,25},{17,1},{25,9},{2,18},{10... | collective-permute-start | bytes 983048 | tf_op jit(solution)/shard_map/ppermute | solution.py:161
  22.9 9.2 %collective-permute-start.19 = (bf16[1280,128]{1,0:T(8,128)(2,1)S(1)}, bf16[1280,128]{1,0:T(8,128)(2,1)}, u32[]{:S(2)}, u32[]{:S(2)}) collective-permute-start(bf16[1280,128]{1,0:T(8,128)(2,1)S(1)} %collective-permute-done.15), channel_id=1, source_target_pairs={{2,4},{3,5},{4,6},{5,7},{10,12},{11,13},{12,14},{13,15},{18,20},{1... | collective-permute-start | bytes 983048 | tf_op jit(solution)/shard_map/ppermute | solution.py:507
  24.3 13.6 %collective-permute-start.18 = (bf16[1280,128]{1,0:T(8,128)(2,1)S(1)}, bf16[1280,128]{1,0:T(8,128)(2,1)}, u32[]{:S(2)}, u32[]{:S(2)}) collective-permute-start(bf16[1280,128]{1,0:T(8,128)(2,1)S(1)} %collective-permute-done.14), channel_id=1, source_target_pairs={{2,0},{3,1},{4,2},{5,3},{10,8},{11,9},{12,10},{13,11},{18,16},{19,... | collective-permute-start | bytes 983048 | tf_op jit(solution)/shard_map/ppermute | solution.py:507
  27.8 2.8 %copy-start = (f32[1152,128]{1,0:T(8,128)S(1)}, f32[1152,128]{1,0:T(8,128)}, u32[]{:S(2)}) copy-start(f32[1152,128]{1,0:T(8,128)} %row_scales.1.refs_12_) | copy-start | bytes 1769476
  29.3 11.0 %slice-start = ((bf16[1280,128]{1,0:T(8,128)(2,1)}), bf16[640,128]{1,0:T(8,128)(2,1)S(1)}, s32[]{:S(2)}) async-start(bf16[1280,128]{1,0:T(8,128)(2,1)} %copy-done.7), calls=%async_computation.2 | async-start | bytes 327680 | tf_op jit(solution)/shard_map/slice | solution.py:166
  30.6 22.6 %copy-start.9 = (bf16[1280,128]{1,0:T(8,128)(2,1)}, bf16[1280,128]{1,0:T(8,128)(2,1)S(1)}, u32[]{:S(2)}) copy-start(bf16[1280,128]{1,0:T(8,128)(2,1)S(1)} %collective-permute-done.20.refs_8_) | copy-start | bytes 983044
  30.6 13.5 %collective-permute-start.27 = (f32[1152,128]{1,0:T(8,128)S(1)}, f32[1152,128]{1,0:T(8,128)S(1)}, u32[]{:S(2)}, u32[]{:S(2)}) collective-permute-start(f32[1152,128]{1,0:T(8,128)S(1)} %copy-done), channel_id=1, source_target_pairs={{0,1},{1,0},{2,3},{3,2},{4,5},{5,4},{6,7},{7,6},{8,9},{9,8},{10,11... | collective-permute-start | bytes 1769480 | tf_op jit(solution)/shard_map/ppermute | solution.py:502
  32.0 21.2 %copy-start.10 = (bf16[1280,128]{1,0:T(8,128)(2,1)}, bf16[1280,128]{1,0:T(8,128)(2,1)S(1)}, u32[]{:S(2)}) copy-start(bf16[1280,128]{1,0:T(8,128)(2,1)S(1)} %collective-permute-done.21.refs_9_) | copy-start | bytes 983044
  38.7 9.2 %collective-permute-start.26 = (bf16[1280,128]{1,0:T(8,128)(2,1)}, bf16[1280,128]{1,0:T(8,128)(2,1)S(1)}, u32[]{:S(2)}, u32[]{:S(2)}) collective-permute-start(bf16[1280,128]{1,0:T(8,128)(2,1)} %pad_maximum_fusion.3), channel_id=1, source_target_pairs={{0,8},{8,0},{16,24},{24,16},{1,9},{9,1},{17,25},{25,17},{2,10},{10... | collective-permute-start | bytes 983048 | tf_op jit(solution)/shard_map/ppermute | solution.py:168
  41.1 9.1 %collective-permute-start.25 = (bf16[1280,128]{1,0:T(8,128)(2,1)}, bf16[1280,128]{1,0:T(8,128)(2,1)S(1)}, u32[]{:S(2)}, u32[]{:S(2)}) collective-permute-start(bf16[1280,128]{1,0:T(8,128)(2,1)} %pad_maximum_fusion.2), channel_id=1, source_target_pairs={{0,16},{8,24},{16,0},{24,8},{1,17},{9,25},{17,1},{25,9},{2,18},{10... | collective-permute-start | bytes 983048 | tf_op jit(solution)/shard_map/ppermute | solution.py:168
  41.4 10.7 %collective-permute-start.23 = (bf16[1280,128]{1,0:T(8,128)(2,1)}, bf16[1280,128]{1,0:T(8,128)(2,1)S(1)}, u32[]{:S(2)}, u32[]{:S(2)}) collective-permute-start(bf16[1280,128]{1,0:T(8,128)(2,1)} %collective-permute-done.18), channel_id=1, source_target_pairs={{2,0},{3,1},{10,8},{11,9},{18,16},{19,17},{26,24},{27,25}} | collective-permute-start | bytes 983048 | tf_op jit(solution)/shard_map/ppermute | solution.py:507
  42.7 9.4 %collective-permute-start.24 = (bf16[1280,128]{1,0:T(8,128)(2,1)}, bf16[1280,128]{1,0:T(8,128)(2,1)}, u32[]{:S(2)}, u32[]{:S(2)}) collective-permute-start(bf16[1280,128]{1,0:T(8,128)(2,1)} %collective-permute-done.19), channel_id=1, source_target_pairs={{4,6},{5,7},{12,14},{13,15},{20,22},{21,23},{28,30},{29,31}} | collective-permute-start | bytes 983048 | tf_op jit(solution)/shard_map/ppermute | solution.py:507
  44.1 11.3 %copy-start.15 = (s32[1,8]{1,0:T(1,128)S(1)}, s32[1,8]{1,0:T(1,128)}, u32[]{:S(2)}) copy-start(s32[1,8]{1,0:T(1,128)} %param.10) | copy-start | bytes 100
  44.1 9.2 %copy-start.3 = (f32[1152,128]{1,0:T(8,128)}, f32[1152,128]{1,0:T(8,128)S(1)}, u32[]{:S(2)}) copy-start(f32[1152,128]{1,0:T(8,128)S(1)} %collective-permute-done.27.refs_13_) | copy-start | bytes 1769476
  47.9 5.4 %copy-start.11 = (bf16[1280,128]{1,0:T(8,128)(2,1)}, bf16[1280,128]{1,0:T(8,128)(2,1)S(1)}, u32[]{:S(2)}) copy-start(bf16[1280,128]{1,0:T(8,128)(2,1)S(1)} %collective-permute-done.26.refs_11_) | copy-start | bytes 983044
  50.2 3.2 %copy-start.12 = (bf16[1280,128]{1,0:T(8,128)(2,1)}, bf16[1280,128]{1,0:T(8,128)(2,1)S(1)}, u32[]{:S(2)}) copy-start(bf16[1280,128]{1,0:T(8,128)(2,1)S(1)} %collective-permute-done.25.refs_10_) | copy-start | bytes 983044
  53.2 17.5 %copy-start.1 = (bf16[1280,128]{1,0:T(8,128)(2,1)}, bf16[1280,128]{1,0:T(8,128)(2,1)S(1)}, u32[]{:S(2)}) copy-start(bf16[1280,128]{1,0:T(8,128)(2,1)S(1)} %get-tuple-element.105.refs_4_) | copy-start | bytes 983044
  53.3 17.5 %copy-start.2 = (bf16[1280,128]{1,0:T(8,128)(2,1)}, bf16[1280,128]{1,0:T(8,128)(2,1)S(1)}, u32[]{:S(2)}) copy-start(bf16[1280,128]{1,0:T(8,128)(2,1)S(1)} %get-tuple-element.106.refs_7_) | copy-start | bytes 983044
  53.3 17.4 %collective-permute-start.28 = (bf16[2560,128]{1,0:T(8,128)(2,1)S(1)}, bf16[2560,128]{1,0:T(8,128)(2,1)S(1)}, u32[]{:S(2)}, u32[]{:S(2)}) collective-permute-start(bf16[2560,128]{1,0:T(8,128)(2,1)S(1)} %pad_maximum_fusion.1), channel_id=1, source_target_pairs={{0,8},{8,0},{16,24},{24,16},{1,9},{9,1},{17,25},{25,17},{2,10},{10... | collective-permute-start | bytes 1966088 | tf_op jit(solution)/shard_map/ppermute | solution.py:161
  53.7 17.1 %collective-permute-start.29 = (bf16[2560,128]{1,0:T(8,128)(2,1)S(1)}, bf16[2560,128]{1,0:T(8,128)(2,1)}, u32[]{:S(2)}, u32[]{:S(2)}) collective-permute-start(bf16[2560,128]{1,0:T(8,128)(2,1)S(1)} %pad_maximum_fusion.1), channel_id=1, source_target_pairs={{0,16},{8,24},{16,0},{24,8},{1,17},{9,25},{17,1},{25,9},{2,18},{10... | collective-permute-start | bytes 1966088 | tf_op jit(solution)/shard_map/ppermute | solution.py:161
  70.8 30.1 %all-to-all-start = ((bf16[8,2,2,128,128]{4,3,2,1,0:T(8,128)(2,1)}), bf16[8,2,2,128,128]{4,3,2,1,0:T(8,128)(2,1)S(1)}, u32[]{:S(2)}, u32[]{:S(2)}) async-start(bf16[8,2,2,128,128]{4,3,2,1,0:T(8,128)(2,1)} %get-tuple-element.84), calls=%async_computation | async-start | bytes 2097152 | tf_op jit(solution)/shard_map/all_to_all | solution.py:464
  75.5 10.1 %collective-permute-start.31 = (bf16[1280,128]{1,0:T(8,128)(2,1)S(1)}, bf16[1280,128]{1,0:T(8,128)(2,1)S(1)}, u32[]{:S(2)}, u32[]{:S(2)}) collective-permute-start(bf16[1280,128]{1,0:T(8,128)(2,1)S(1)} %pad_maximum_fusion.5), channel_id=1, source_target_pairs={{0,8},{8,0},{16,24},{24,16},{1,9},{9,1},{17,25},{25,17},{2,10},{10... | collective-permute-start | bytes 983048 | tf_op jit(solution)/shard_map/ppermute | solution.py:168
  75.6 10.1 %collective-permute-start.30 = (bf16[1280,128]{1,0:T(8,128)(2,1)S(1)}, bf16[1280,128]{1,0:T(8,128)(2,1)S(1)}, u32[]{:S(2)}, u32[]{:S(2)}) collective-permute-start(bf16[1280,128]{1,0:T(8,128)(2,1)S(1)} %pad_maximum_fusion.4), channel_id=1, source_target_pairs={{0,16},{8,24},{16,0},{24,8},{1,17},{9,25},{17,1},{25,9},{2,18},{10... | collective-permute-start | bytes 983048 | tf_op jit(solution)/shard_map/ppermute | solution.py:168
  85.6 0.7 copy-start.13
  85.7 0.7 copy-start.14
  100.9 30.1 %all-to-all-start.1 = ((bf16[8,2,2,128,128]{4,3,2,1,0:T(8,128)(2,1)}), bf16[8,2,2,128,128]{4,3,2,1,0:T(8,128)(2,1)S(1)}, u32[]{:S(2)}, u32[]{:S(2)}) async-start(bf16[8,2,2,128,128]{4,3,2,1,0:T(8,128)(2,1)} %get-tuple-element.89), calls=%async_computation.1 | async-start | bytes 2097152 | tf_op jit(solution)/shard_map/all_to_all | solution.py:464
  132.5 1.1 copy-start.6
